TPU v7x, 32 devices: a whole 2x2x4 slice. The times are simulated.
32 devices in a mesh: shot: 2 (over x), gx: 16 (over z, y, core).
Axes of the slice: x: 2, y: 2, z: 4, core: 2. Of those that a mesh axis runs over, the one named last changes fastest.
Arguments:
- fwd_fields: float32 [6, 256, 64, 512], P(None, ('shot', 'gx')), parts along dimension 1, may hold values from -6 to 6
- velocity: float32 [128, 64, 512], P('gx'), may hold values from 1.5 to 4.4
- adj_prev: float32 [256, 64, 512], P(('shot', 'gx')), parts along dimension 0, may hold values from -8 to 20
- adj_now: float32 [256, 64, 512], P(('shot', 'gx')), parts along dimension 0, may hold values from -8 to 20
- residual: float32 [4, 8192], P(None, ('shot', 'gx')), parts along dimension 1, may hold values from -6 to 6
- rec_owner: int32 [4096, 1], P('gx'), may hold values from 0 to 15; in each aligned block of 256 rows (0 to 255, 256 to 511, ...) at most 16 rows name the same one
- rec_cell: int32 [4096], P('gx'), may hold values from 0 to 262143
- rec_cluster: int32 [4096], P('gx'), may hold values from 0 to 31
- cluster_gain: float32 [32], replicated, may hold values from 0.5 to 2
Outputs:
- adjoint_older: float32 [256, 64, 512], P(('shot', 'gx')), parts along dimension 0
- adjoint_newer: float32 [256, 64, 512], P(('shot', 'gx')), parts along dimension 0
- gradient: float32 [256, 64, 512], P(('shot', 'gx')), parts along dimension 0
There are 2 independent parts, one for each index of `shot`. A program takes and returns all parts, laid end to end along the dimension named above; an argument that names none is the same for every part. Nothing has to cross between parts.
Inputs may be any that keep to these rules, and one draw needn't show every extreme that they name: `rec_owner`: among the traces of one device (aligned blocks of 256 rows) at most 16 name the same block; some block is named by exactly 16 of them.
All inputs are finite; a program needn't handle non-finite values.
Results may differ from a plain program's by a relative error of at most 0.00002.
Values sent between devices are 32-bit elements; how exact they have to be, the bound alone decides.
A program may use at most 64 MiB of HBM per device.

v0:
```python
import jax
import jax.numpy as jnp
from jax import lax
from jax.sharding import PartitionSpec as P

STEPS = 4
CAP = 16


stencil_weights = (-205.0 / 72.0, 8.0 / 5.0, -1.0 / 5.0, 8.0 / 315.0, -1.0 / 560.0)
time_ratio = 0.1


def with_halo(shard, sides, width):
    for axis, dim in sides:
        devices, length = (lax.axis_size(axis), shard.shape[dim])
        up = [(i, (i + 1) % devices) for i in range(devices - 1)]
        down = [(j, i) for i, j in up]
        last = lax.slice_in_dim(shard, length - width, length, axis=dim)
        initial = lax.slice_in_dim(shard, 0, width, axis=dim)
        before = lax.ppermute(last, axis, up)
        after = lax.ppermute(initial, axis, down)
        shard = jnp.concatenate([before, shard, after], axis=dim)
    return shard


def laplace(extended):
    row_count = extended.shape[0] - 8
    centre = extended[4 : 4 + row_count]
    depth_cells = centre.shape[1]
    cross_cells = centre.shape[2]
    summed = 3.0 * stencil_weights[0] * centre
    for offset in range(1, 5):
        summed = summed + stencil_weights[offset] * (
            extended[4 + offset : 4 + offset + row_count]
            + extended[4 - offset : 4 - offset + row_count]
        )
    padded_z = jnp.pad(centre, ((0, 0), (4, 4), (0, 0)))
    for offset in range(1, 5):
        summed = summed + stencil_weights[offset] * (
            padded_z[:, 4 + offset : 4 + offset + depth_cells]
            + padded_z[:, 4 - offset : 4 - offset + depth_cells]
        )
    padded_y = jnp.pad(centre, ((0, 0), (0, 0), (4, 4)))
    for offset in range(1, 5):
        summed = summed + stencil_weights[offset] * (
            padded_y[:, :, 4 + offset : 4 + offset + cross_cells]
            + padded_y[:, :, 4 - offset : 4 - offset + cross_cells]
        )
    return summed


def inject(wave_field, cells_in, values):
    flat = wave_field.reshape(-1).at[cells_in].add(values)
    return flat.reshape(wave_field.shape)


def per_device(
    fwd_fields,
    velocity,
    adj_prev,
    adj_now,
    residual,
    rec_owner,
    rec_cell,
    rec_cluster,
    cluster_gain,
):
    devices = lax.axis_size("gx")
    courant = jnp.square(time_ratio * velocity)
    scaling = 2.0 / velocity
    picked = rec_cluster[:, None] == jnp.arange(cluster_gain.shape[0], dtype=jnp.int32)[None, :]
    gains = jnp.sum(jnp.where(picked, cluster_gain[None, :], 0.0), axis=1)
    amplitude = residual * gains[None, :]
    owner = rec_owner[:, 0]
    member = (owner[:, None] == jnp.arange(devices, dtype=jnp.int32)[None, :]).astype(jnp.int32)
    ranked = jnp.cumsum(member, axis=0) - 1
    slot_index = jnp.sum(member * ranked, axis=1)
    target = owner * CAP + slot_index
    send_cells = (
        jnp.zeros((devices * CAP,), jnp.int32).at[target].set(rec_cell).reshape(devices, CAP)
    )
    send_values = (
        jnp.zeros((devices * CAP, STEPS), jnp.float32)
        .at[target]
        .set(amplitude.T)
        .reshape(devices, CAP, STEPS)
    )
    older = adj_prev
    newer = adj_now
    image = jnp.zeros_like(adj_now)
    for step in range(STEPS):
        image = image + scaling * newer * (
            fwd_fields[step] - 2.0 * fwd_fields[step + 1] + fwd_fields[step + 2]
        )
        extended = with_halo(newer, (("gx", 0),), 4)
        following = 2.0 * newer - older + courant * laplace(extended)
        got_cells = lax.all_to_all(send_cells, "gx", split_axis=0, concat_axis=0, tiled=True)
        got_values = lax.all_to_all(
            send_values[:, :, step], "gx", split_axis=0, concat_axis=0, tiled=True
        )
        cells_in = got_cells.reshape(-1)
        values_in = got_values.reshape(-1)
        following = inject(following, cells_in, values_in)
        older = newer
        newer = following
    return (older, newer, image)


def solution(mesh):
    in_specs = (
        P(None, ("shot", "gx"), None, None),
        P("gx", None, None),
        P(("shot", "gx"), None, None),
        P(("shot", "gx"), None, None),
        P(None, ("shot", "gx")),
        P("gx", None),
        P("gx"),
        P("gx"),
        P(),
    )
    out_specs = (
        P(("shot", "gx"), None, None),
        P(("shot", "gx"), None, None),
        P(("shot", "gx"), None, None),
    )
    return jax.shard_map(
        per_device, mesh=mesh, in_specs=in_specs, out_specs=out_specs, check_vma=False
    )
```

profile of v0, /device:TPU:9, one launch (start us, length us, event | category | flops | bytes accessed | tf_op | source)
XLA Modules:
  0.0 147.3 jit_solution(5973937151339991899)
XLA Ops:
  5.9 6.6 %all-to-all-start = ((s32[16,1,16]{2,1,0:T(1,128)}), s32[16,1,16]{2,1,0:T(1,128)S(1)}, u32[]{:S(2)}, u32[]{:S(2)}) async-start(s32[16,1,16]{2,1,0:T(1,128)} %all_to_all.33), calls=%async_computation | async-start | bytes 16384 | tf_op jit(solution)/shard_map/all_to_all | solution.py:98
  12.5 2.1 %fusion.157 = (f32[4,64,512]{2,1,0:T(8,128)S(1)}, f32[4,64,512]{2,1,0:T(8,128)}) fusion(f32[8,64,512]{2,1,0:T(8,128)} %param.12), kind=kLoop, calls=%fused_computation.278 | loop fusion | bytes 2097152 | tf_op jit(solution)/shard_map/slice | solution.py:20
  14.6 2.4 %collective-permute-start = (f32[4,64,512]{2,1,0:T(8,128)S(1)}, f32[4,64,512]{2,1,0:T(8,128)S(1)}, u32[]{:S(2)}, u32[]{:S(2)}) collective-permute-start(f32[4,64,512]{2,1,0:T(8,128)S(1)} %get-tuple-element.16), channel_id=1, source_target_pairs={{1,0},{2,1},{3,2},{4,3},{5,4},{6,5},{7,6},{8,7},{9,8},{10,9},{11,1... | collective-permute-start | bytes 1572872 | tf_op jit(solution)/shard_map/ppermute | solution.py:22
  17.0 3.3 %collective-permute-start.1 = (f32[4,64,512]{2,1,0:T(8,128)}, f32[4,64,512]{2,1,0:T(8,128)S(1)}, u32[]{:S(2)}, u32[]{:S(2)}) collective-permute-start(f32[4,64,512]{2,1,0:T(8,128)} %get-tuple-element.17), channel_id=1, source_target_pairs={{0,1},{1,2},{2,3},{3,4},{4,5},{5,6},{6,7},{7,8},{8,9},{9,10},{10,1... | collective-permute-start | bytes 1572872 | tf_op jit(solution)/shard_map/ppermute | solution.py:21
  22.7 5.8 %all-to-all-start.1 = ((f32[16,1,16]{2,1,0:T(1,128)}), f32[16,1,16]{2,1,0:T(1,128)S(1)}, u32[]{:S(2)}, u32[]{:S(2)}) async-start(f32[16,1,16]{2,1,0:T(1,128)} %bitcast.9), calls=%async_computation.1 | async-start | bytes 16384 | tf_op jit(solution)/shard_map/all_to_all | solution.py:99
  29.7 3.3 %all-to-all-done.1 = f32[16,1,16]{2,1,0:T(1,128)S(1)} async-done(((f32[16,1,16]{2,1,0:T(1,128)}), f32[16,1,16]{2,1,0:T(1,128)S(1)}, u32[]{:S(2)}, u32[]{:S(2)}) %all-to-all-start.1) | async-done | bytes 1056 | tf_op jit(solution)/shard_map/all_to_all | solution.py:99
  35.9 2.5 %fusion.11 = f32[8,64,512]{2,1,0:T(8,128)S(1)} fusion(f32[8,64,512]{2,1,0:T(8,128)S(1)} %copy-done, f32[12,64,512]{2,1,0:T(8,128)S(1)} %get-tuple-element.19, f32[12,64,512]{2,1,0:T(8,128)S(1)} %constant_dynamic-update-slice_fusion, f32[8,64,512]{2,1,0:T(8,128)S(1)} %copy-done.6, f32[8,64,512]{2,1,0:T(8,128)S(1)} %copy-done.1), kind=kLoop, calls=%fused_computation.81 | loop fusion | flops 11272192 | bytes 12582912 | tf_op jit(solution)/shard_map/add | solution.py:97
  38.7 2.3 %scatter_fusion = f32[262144]{0:T(1024)S(1)} fusion(f32[262144]{0:T(1024)S(1)} %bitcast.99, s32[256]{0:T(256)S(1)} %bitcast.111, f32[256]{0:T(256)S(1)} %reshape.211), kind=kCustom, calls=%fused_computation.2 | custom fusion | flops 256 | bytes 4096 | tf_op jit(solution)/shard_map/scatter-add | solution.py:54
  44.1 2.7 %collective-permute-start.3 = (f32[4,64,512]{2,1,0:T(8,128)}, f32[4,64,512]{2,1,0:T(8,128)}, u32[]{:S(2)}, u32[]{:S(2)}) collective-permute-start(f32[4,64,512]{2,1,0:T(8,128)} %slice.485), channel_id=1, source_target_pairs={{0,1},{1,2},{2,3},{3,4},{4,5},{5,6},{6,7},{7,8},{8,9},{9,10},{10,1... | collective-permute-start | bytes 1572872 | tf_op jit(solution)/shard_map/ppermute | solution.py:21
  46.9 1.9 %slice.482 = f32[4,64,512]{2,1,0:T(8,128)} reshape(f32[131072]{0:T(1024)} %get-tuple-element.12) | data formatting | bytes 1048576 | tf_op jit(solution)/shard_map/slice | solution.py:20
  48.8 1.9 %collective-permute-start.2 = (f32[4,64,512]{2,1,0:T(8,128)}, f32[4,64,512]{2,1,0:T(8,128)}, u32[]{:S(2)}, u32[]{:S(2)}) collective-permute-start(f32[4,64,512]{2,1,0:T(8,128)} %slice.482), channel_id=1, source_target_pairs={{1,0},{2,1},{3,2},{4,3},{5,4},{6,5},{7,6},{8,7},{9,8},{10,9},{11,1... | collective-permute-start | bytes 1572872 | tf_op jit(solution)/shard_map/ppermute | solution.py:22
  50.9 10.6 %all_to_all.48 = f32[16,1,16]{2,1,0:T(1,128)S(1)} all-to-all(f32[16,1,16]{2,1,0:T(1,128)S(1)} %bitcast.108), channel_id=1, replica_groups=mesh['shot'=2,'gx'=16] {'gx'}, dimensions={0} | all-to-all | bytes 2048 | tf_op jit(solution)/shard_map/all_to_all | solution.py:99
  66.1 2.5 %fusion.29 = f32[8,64,512]{2,1,0:T(8,128)S(1)} fusion(f32[8,64,512]{2,1,0:T(8,128)S(1)} %reshape.181, f32[12,64,512]{2,1,0:T(8,128)S(1)} %get-tuple-element.15, f32[12,64,512]{2,1,0:T(8,128)S(1)} %constant_dynamic-update-slice_fusion.4, f32[8,64,512]{2,1,0:T(8,128)S(1)} %copy-done, f32[8,64,512]{2,1,0:T(8,128)S(1)} %copy-done.1), kind=kLoop, calls=%fused_computation.99 | loop fusion | flops 11272192 | bytes 12582912 | tf_op jit(solution)/shard_map/add | solution.py:97
  69.8 4.1 %scatter_fusion.1 = f32[262144]{0:T(1024)} fusion(f32[262144]{0:T(1024)} %bitcast.100, s32[256]{0:T(256)S(1)} %bitcast.112, f32[256]{0:T(256)S(1)} %reshape.219), kind=kCustom, calls=%fused_computation.3 | custom fusion | flops 256 | bytes 4096 | tf_op jit(solution)/shard_map/scatter-add | solution.py:54
  73.9 2.2 %fusion.155 = (f32[131072]{0:T(1024)}, f32[131072]{0:T(1024)}) fusion(f32[262144]{0:T(1024)} %scatter_fusion.1), kind=kLoop, calls=%fused_computation.276 | loop fusion | bytes 2097152 | tf_op jit(solution)/shard_map/slice | solution.py:20
  78.1 2.7 %collective-permute-start.5 = (f32[4,64,512]{2,1,0:T(8,128)}, f32[4,64,512]{2,1,0:T(8,128)}, u32[]{:S(2)}, u32[]{:S(2)}) collective-permute-start(f32[4,64,512]{2,1,0:T(8,128)} %slice.514), channel_id=1, source_target_pairs={{0,1},{1,2},{2,3},{3,4},{4,5},{5,6},{6,7},{7,8},{8,9},{9,10},{10,1... | collective-permute-start | bytes 1572872 | tf_op jit(solution)/shard_map/ppermute | solution.py:21
  80.7 1.9 %slice.511 = f32[4,64,512]{2,1,0:T(8,128)} reshape(f32[131072]{0:T(1024)} %get-tuple-element.8) | data formatting | bytes 1048576 | tf_op jit(solution)/shard_map/slice | solution.py:20
  82.6 1.9 %collective-permute-start.4 = (f32[4,64,512]{2,1,0:T(8,128)}, f32[4,64,512]{2,1,0:T(8,128)}, u32[]{:S(2)}, u32[]{:S(2)}) collective-permute-start(f32[4,64,512]{2,1,0:T(8,128)} %slice.511), channel_id=1, source_target_pairs={{1,0},{2,1},{3,2},{4,3},{5,4},{6,5},{7,6},{8,7},{9,8},{10,9},{11,1... | collective-permute-start | bytes 1572872 | tf_op jit(solution)/shard_map/ppermute | solution.py:22
  84.7 10.6 %all_to_all.49 = f32[16,1,16]{2,1,0:T(1,128)S(1)} all-to-all(f32[16,1,16]{2,1,0:T(1,128)S(1)} %bitcast.109), channel_id=1, replica_groups=mesh['shot'=2,'gx'=16] {'gx'}, dimensions={0} | all-to-all | bytes 2048 | tf_op jit(solution)/shard_map/all_to_all | solution.py:99
  96.0 2.4 %reshape.184 = f32[8,64,512]{2,1,0:T(8,128)} reshape(f32[262144]{0:T(1024)} %scatter_fusion.1) | data formatting | bytes 2097152 | tf_op jit(solution)/shard_map/reshape | solution.py:55
  101.1 2.6 %fusion.47 = f32[8,64,512]{2,1,0:T(8,128)S(1)} fusion(f32[8,64,512]{2,1,0:T(8,128)S(1)} %copy-done.2, f32[12,64,512]{2,1,0:T(8,128)S(1)} %get-tuple-element.11, f32[12,64,512]{2,1,0:T(8,128)S(1)} %constant_dynamic-update-slice_fusion.8, f32[8,64,512]{2,1,0:T(8,128)S(1)} %reshape.181, f32[8,64,512]{2,1,0:T(8,128)S(1)} %copy-done.1), kind=kLoop, calls=%fused_computation.117 | loop fusion | flops 11272192 | bytes 12582912 | tf_op jit(solution)/shard_map/add | solution.py:97
  105.0 4.1 %scatter_fusion.2 = f32[262144]{0:T(1024)} fusion(f32[262144]{0:T(1024)} %bitcast.101, s32[256]{0:T(256)S(1)} %bitcast.113, f32[256]{0:T(256)S(1)} %reshape.227), kind=kCustom, calls=%fused_computation.4 | custom fusion | flops 256 | bytes 4096 | tf_op jit(solution)/shard_map/scatter-add | solution.py:54
  109.1 2.2 %fusion.154 = (f32[131072]{0:T(1024)}, f32[131072]{0:T(1024)}) fusion(f32[262144]{0:T(1024)} %scatter_fusion.2), kind=kLoop, calls=%fused_computation.275 | loop fusion | bytes 2097152 | tf_op jit(solution)/shard_map/slice | solution.py:20
  111.3 1.9 %slice.543 = f32[4,64,512]{2,1,0:T(8,128)} reshape(f32[131072]{0:T(1024)} %get-tuple-element.7) | data formatting | bytes 1048576 | tf_op jit(solution)/shard_map/slice | solution.py:19
  113.2 2.7 %collective-permute-start.7 = (f32[4,64,512]{2,1,0:T(8,128)}, f32[4,64,512]{2,1,0:T(8,128)}, u32[]{:S(2)}, u32[]{:S(2)}) collective-permute-start(f32[4,64,512]{2,1,0:T(8,128)} %slice.543), channel_id=1, source_target_pairs={{0,1},{1,2},{2,3},{3,4},{4,5},{5,6},{6,7},{7,8},{8,9},{9,10},{10,1... | collective-permute-start | bytes 1572872 | tf_op jit(solution)/shard_map/ppermute | solution.py:21
  116.1 9.1 %all_to_all.50 = f32[16,1,16]{2,1,0:T(1,128)S(1)} all-to-all(f32[16,1,16]{2,1,0:T(1,128)S(1)} %bitcast.110), channel_id=1, replica_groups=mesh['shot'=2,'gx'=16] {'gx'}, dimensions={0} | all-to-all | bytes 2048 | tf_op jit(solution)/shard_map/all_to_all | solution.py:99
  125.9 2.4 %reshape.187 = f32[8,64,512]{2,1,0:T(8,128)} reshape(f32[262144]{0:T(1024)} %scatter_fusion.2) | data formatting | bytes 2097152 | tf_op jit(solution)/shard_map/reshape | solution.py:55
  128.2 1.9 %slice.540 = f32[4,64,512]{2,1,0:T(8,128)} reshape(f32[131072]{0:T(1024)} %get-tuple-element.6) | data formatting | bytes 1048576 | tf_op jit(solution)/shard_map/slice | solution.py:20
  130.1 2.5 %collective-permute-start.6 = (f32[4,64,512]{2,1,0:T(8,128)}, f32[4,64,512]{2,1,0:T(8,128)S(1)}, u32[]{:S(2)}, u32[]{:S(2)}) collective-permute-start(f32[4,64,512]{2,1,0:T(8,128)} %slice.540), channel_id=1, source_target_pairs={{1,0},{2,1},{3,2},{4,3},{5,4},{6,5},{7,6},{8,7},{9,8},{10,9},{11,1... | collective-permute-start | bytes 1572872 | tf_op jit(solution)/shard_map/ppermute | solution.py:22
  133.7 5.6 %fusion.137 = (f32[8,64,512]{2,1,0:T(8,128)}, f32[12,64,512]{2,1,0:T(8,128)S(1)}, f32[12,64,512]{2,1,0:T(8,128)S(1)}) fusion(f32[6,8,64,512]{3,2,1,0:T(8,128)} %param.9, f32[8,64,512]{2,1,0:T(8,128)} %reshape.187, f32[8,64,512]{2,1,0:T(8,128)S(1)} %copy-done.3, f32[8,64,512]{2,1,0:T(8,128)S(1)} %reshape.181, f32[8,64,512]{2,1,0:T(8,128)S(1)} %copy-done, ...), kind=kLoop, calls=%fused_computation.224 | loop fusion | flops 6291455 | bytes 14680064 | tf_op jit(solution)/shard_map/add | solution.py:93
  141.0 2.5 %fusion.65 = f32[8,64,512]{2,1,0:T(8,128)S(1)} fusion(f32[8,64,512]{2,1,0:T(8,128)S(1)} %copy-done.5, f32[12,64,512]{2,1,0:T(8,128)S(1)} %get-tuple-element.4, f32[12,64,512]{2,1,0:T(8,128)S(1)} %constant_dynamic-update-slice_fusion.12, f32[8,64,512]{2,1,0:T(8,128)S(1)} %copy-done.3, f32[8,64,512]{2,1,0:T(8,128)S(1)} %copy-done.1), kind=kLoop, calls=%fused_computation.135 | loop fusion | flops 11272192 | bytes 12582912 | tf_op jit(solution)/shard_map/add | solution.py:97
  143.8 2.3 %scatter_fusion.3 = f32[262144]{0:T(1024)S(1)} fusion(f32[262144]{0:T(1024)S(1)} %bitcast.102, s32[256]{0:T(256)S(1)} %bitcast.114, f32[256]{0:T(256)S(1)} %reshape.235), kind=kCustom, calls=%fused_computation.5 | custom fusion | flops 256 | bytes 4096 | tf_op jit(solution)/shard_map/scatter-add | solution.py:54
  (80 shorter events, 32.6 us)
Async XLA Ops:
  0.6 19.6 %copy-start.9 = (f32[32]{0:T(128)S(1)}, f32[32]{0:T(128)}, u32[]{:S(2)}) copy-start(f32[32]{0:T(128)} %param.17) | copy-start | bytes 388
  0.6 19.6 %copy-start.8 = (s32[256]{0:T(256)S(1)}, s32[256]{0:T(256)}, u32[]{:S(2)}) copy-start(s32[256]{0:T(256)} %param.16) | copy-start | bytes 3076
  0.7 19.7 %copy-start.7 = (f32[4,256]{1,0:T(4,128)S(1)}, f32[4,256]{1,0:T(4,128)}, u32[]{:S(2)}) copy-start(f32[4,256]{1,0:T(4,128)} %param.13) | copy-start | bytes 12292
  5.9 16.8 %all-to-all-start = ((s32[16,1,16]{2,1,0:T(1,128)}), s32[16,1,16]{2,1,0:T(1,128)S(1)}, u32[]{:S(2)}, u32[]{:S(2)}) async-start(s32[16,1,16]{2,1,0:T(1,128)} %all_to_all.33), calls=%async_computation | async-start | bytes 16384 | tf_op jit(solution)/shard_map/all_to_all | solution.py:98
  14.6 19.8 %copy-start = (f32[8,64,512]{2,1,0:T(8,128)S(1)}, f32[8,64,512]{2,1,0:T(8,128)}, u32[]{:S(2)}) copy-start(f32[8,64,512]{2,1,0:T(8,128)} %param.12) | copy-start | bytes 3145732
  14.6 20.1 %collective-permute-start = (f32[4,64,512]{2,1,0:T(8,128)S(1)}, f32[4,64,512]{2,1,0:T(8,128)S(1)}, u32[]{:S(2)}, u32[]{:S(2)}) collective-permute-start(f32[4,64,512]{2,1,0:T(8,128)S(1)} %get-tuple-element.16), channel_id=1, source_target_pairs={{1,0},{2,1},{3,2},{4,3},{5,4},{6,5},{7,6},{8,7},{9,8},{10,9},{11,1... | collective-permute-start | bytes 1572872 | tf_op jit(solution)/shard_map/ppermute | solution.py:22
  17.0 17.3 %collective-permute-start.1 = (f32[4,64,512]{2,1,0:T(8,128)}, f32[4,64,512]{2,1,0:T(8,128)S(1)}, u32[]{:S(2)}, u32[]{:S(2)}) collective-permute-start(f32[4,64,512]{2,1,0:T(8,128)} %get-tuple-element.17), channel_id=1, source_target_pairs={{0,1},{1,2},{2,3},{3,4},{4,5},{5,6},{6,7},{7,8},{8,9},{9,10},{10,1... | collective-permute-start | bytes 1572872 | tf_op jit(solution)/shard_map/ppermute | solution.py:21
  22.7 10.4 %all-to-all-start.1 = ((f32[16,1,16]{2,1,0:T(1,128)}), f32[16,1,16]{2,1,0:T(1,128)S(1)}, u32[]{:S(2)}, u32[]{:S(2)}) async-start(f32[16,1,16]{2,1,0:T(1,128)} %bitcast.9), calls=%async_computation.1 | async-start | bytes 16384 | tf_op jit(solution)/shard_map/all_to_all | solution.py:99
  34.4 1.2 copy-start.1
  34.4 1.5 %copy-start.6 = (f32[8,64,512]{2,1,0:T(8,128)S(1)}, f32[8,64,512]{2,1,0:T(8,128)}, u32[]{:S(2)}) copy-start(f32[8,64,512]{2,1,0:T(8,128)} %param.11) | copy-start | bytes 3145732
  41.0 3.1 %copy-start.4 = (f32[262144]{0:T(1024)}, f32[262144]{0:T(1024)S(1)}, u32[]{:S(2)}) copy-start(f32[262144]{0:T(1024)S(1)} %scatter_fusion) | copy-start | bytes 3145732
  44.1 19.5 %collective-permute-start.3 = (f32[4,64,512]{2,1,0:T(8,128)}, f32[4,64,512]{2,1,0:T(8,128)}, u32[]{:S(2)}, u32[]{:S(2)}) collective-permute-start(f32[4,64,512]{2,1,0:T(8,128)} %slice.485), channel_id=1, source_target_pairs={{0,1},{1,2},{2,3},{3,4},{4,5},{5,6},{6,7},{7,8},{8,9},{9,10},{10,1... | collective-permute-start | bytes 1572872 | tf_op jit(solution)/shard_map/ppermute | solution.py:21
  48.8 16.2 %collective-permute-start.2 = (f32[4,64,512]{2,1,0:T(8,128)}, f32[4,64,512]{2,1,0:T(8,128)}, u32[]{:S(2)}, u32[]{:S(2)}) collective-permute-start(f32[4,64,512]{2,1,0:T(8,128)} %slice.482), channel_id=1, source_target_pairs={{1,0},{2,1},{3,2},{4,3},{5,4},{6,5},{7,6},{8,7},{9,8},{10,9},{11,1... | collective-permute-start | bytes 1572872 | tf_op jit(solution)/shard_map/ppermute | solution.py:22
  78.1 20.3 %collective-permute-start.5 = (f32[4,64,512]{2,1,0:T(8,128)}, f32[4,64,512]{2,1,0:T(8,128)}, u32[]{:S(2)}, u32[]{:S(2)}) collective-permute-start(f32[4,64,512]{2,1,0:T(8,128)} %slice.514), channel_id=1, source_target_pairs={{0,1},{1,2},{2,3},{3,4},{4,5},{5,6},{6,7},{7,8},{8,9},{9,10},{10,1... | collective-permute-start | bytes 1572872 | tf_op jit(solution)/shard_map/ppermute | solution.py:21
  82.6 17.4 %collective-permute-start.4 = (f32[4,64,512]{2,1,0:T(8,128)}, f32[4,64,512]{2,1,0:T(8,128)}, u32[]{:S(2)}, u32[]{:S(2)}) collective-permute-start(f32[4,64,512]{2,1,0:T(8,128)} %slice.511), channel_id=1, source_target_pairs={{1,0},{2,1},{3,2},{4,3},{5,4},{6,5},{7,6},{8,7},{9,8},{10,9},{11,1... | collective-permute-start | bytes 1572872 | tf_op jit(solution)/shard_map/ppermute | solution.py:22
  98.4 1.4 copy-start.2
  113.2 19.4 %collective-permute-start.7 = (f32[4,64,512]{2,1,0:T(8,128)}, f32[4,64,512]{2,1,0:T(8,128)}, u32[]{:S(2)}, u32[]{:S(2)}) collective-permute-start(f32[4,64,512]{2,1,0:T(8,128)} %slice.543), channel_id=1, source_target_pairs={{0,1},{1,2},{2,3},{3,4},{4,5},{5,6},{6,7},{7,8},{8,9},{9,10},{10,1... | collective-permute-start | bytes 1572872 | tf_op jit(solution)/shard_map/ppermute | solution.py:21
  130.1 3.6 %copy-start.3 = (f32[8,64,512]{2,1,0:T(8,128)S(1)}, f32[8,64,512]{2,1,0:T(8,128)}, u32[]{:S(2)}) copy-start(f32[8,64,512]{2,1,0:T(8,128)} %reshape.184) | copy-start | bytes 3145732
  130.1 10.8 %collective-permute-start.6 = (f32[4,64,512]{2,1,0:T(8,128)}, f32[4,64,512]{2,1,0:T(8,128)S(1)}, u32[]{:S(2)}, u32[]{:S(2)}) collective-permute-start(f32[4,64,512]{2,1,0:T(8,128)} %slice.540), channel_id=1, source_target_pairs={{1,0},{2,1},{3,2},{4,3},{5,4},{6,5},{7,6},{8,7},{9,8},{10,9},{11,1... | collective-permute-start | bytes 1572872 | tf_op jit(solution)/shard_map/ppermute | solution.py:22
  139.4 1.7 %copy-start.5 = (f32[8,64,512]{2,1,0:T(8,128)S(1)}, f32[8,64,512]{2,1,0:T(8,128)}, u32[]{:S(2)}) copy-start(f32[8,64,512]{2,1,0:T(8,128)} %reshape.187) | copy-start | bytes 3145732
where the time goes:
time: 150 us; the launch traced here: 147 us
  local copies, waits for them, and re-layouts  43.8 us (29%)
  other arithmetic  34.6 us (23%)
  starting transfers between devices  32.4 us (22%)
  blocking collectives  30.4 us (20%)
  waiting for transfers between devices  4.99 us (3%)
    all_to_all x3, blocking collectives, per_device(): lax.all_to_all(send_values[:, :, step], 'gx', split_axis=0, concat_axis=0...  30.4 us
    slice x7, local copies, waits for them, and re-layouts, with_halo(): initial = lax.slice_in_dim(shard, 0, width, axis=dim)  13.5 us
    scatter-add x4, other arithmetic, inject(): flat = wave_field.reshape(-1).at[cells_in].add(values)  12.9 us
    ppermute x4, starting transfers between devices, with_halo(): before = lax.ppermute(last, axis, up)  11.4 us
    add x4, other arithmetic, per_device(): following = 2.0 * newer - older + courant * laplace(extended)  10.1 us
    unnamed x35, local copies, waits for them, and re-layouts  9.8 us
    ppermute x4, starting transfers between devices, with_halo(): after = lax.ppermute(initial, axis, down)  8.68 us
    reshape x4, local copies, waits for them, and re-layouts, inject(): return flat.reshape(wave_field.shape)  7.24 us
  transfers between devices with their start and end apart: 10, of which 2 were waited for; matrix products, arithmetic and copies ran while one was open for 21% of the time, Pallas kernels for 0%

commit v1 on v0

v1 whole, which is shorter than its diff:
```python
import functools

import jax
import jax.numpy as jnp
from jax import lax
from jax.experimental import pallas as pl
from jax.experimental.pallas import tpu as pltpu
from jax.sharding import PartitionSpec as P

STEPS = 4
CAP = 16
CHUNKS = 4
PAD = 8
HALO = 4
LANES = 128
FIELDS = 6
MESH = pl.DeviceIdType.MESH

stencil_weights = (-205.0 / 72.0, 8.0 / 5.0, -1.0 / 5.0, 8.0 / 315.0, -1.0 / 560.0)
time_ratio = 0.1


def iota(shape, dim):
    return lax.broadcasted_iota(jnp.int32, shape, dim)


def pack_traces(n, residual, owner, cell, cluster, gain, width):
    traces = residual.shape[1]
    clusters = gain.shape[0]
    picked = cluster == iota((clusters, traces), 0)
    gains = jnp.sum(jnp.where(picked, gain, 0.0), axis=0, keepdims=True)
    amplitude = residual * gains
    member = jnp.where(owner == iota((n, traces), 0), 1.0, 0.0)
    upper = jnp.where(iota((traces, traces), 0) <= iota((traces, traces), 1), 1.0, 0.0)
    ranked = jnp.dot(
        member.astype(jnp.bfloat16),
        upper.astype(jnp.bfloat16),
        preferred_element_type=jnp.float32,
    )
    slot = jnp.sum(member * (ranked - 1.0), axis=0, keepdims=True)
    row = cell // width
    column = cell - row * width
    lines = jnp.concatenate(
        [
            amplitude,
            row.astype(jnp.float32),
            column.astype(jnp.float32),
            slot,
            jnp.zeros((LANES - STEPS - 3, traces), jnp.float32),
        ],
        axis=0,
    )
    lines = lines.T
    lane = iota((traces, LANES), 1)
    spread = jnp.zeros((traces, LANES), jnp.float32)
    for field in range(FIELDS):
        spread = jnp.where(lane // CAP == field, lines[:, field : field + 1], spread)
    slots = lines[:, FIELDS : FIELDS + 1].astype(jnp.int32)
    spread = jnp.where(lane % CAP == slots, spread, 0.0)
    return jnp.dot(
        member, spread, precision=lax.Precision.HIGHEST, preferred_element_type=jnp.float32
    )


def kernel(
    n,
    fwd_hbm,
    velocity_hbm,
    prev_hbm,
    now_hbm,
    residual,
    owner,
    cell,
    cluster,
    gain,
    older_hbm,
    newer_hbm,
    image_hbm,
    field,
    fwd,
    velocity,
    image,
    added,
    outbox,
    inbox,
    row_hot,
    columns,
    parts,
    load_sem,
    out_sem,
    send_sem,
    recv_sem,
    mail_send,
    mail_recv,
):
    shot = lax.axis_index("shot")
    me = lax.axis_index("gx")
    layers, depth, width = now_hbm.shape
    rows = depth // CHUNKS
    slots = n * CAP

    barrier = pltpu.get_barrier_semaphore()

    @pl.loop(1, n)
    def _(i):
        pl.semaphore_signal(
            barrier, inc=1, device_id=(shot, lax.rem(me + i, n)), device_id_type=MESH
        )

    loads = [
        pltpu.make_async_copy(
            now_hbm, field.at[1, pl.ds(HALO, layers), pl.ds(PAD, depth), :], load_sem.at[0]
        ),
        pltpu.make_async_copy(
            prev_hbm, field.at[0, pl.ds(HALO, layers), pl.ds(PAD, depth), :], load_sem.at[1]
        ),
        pltpu.make_async_copy(velocity_hbm, velocity, load_sem.at[2]),
        pltpu.make_async_copy(fwd_hbm, fwd, load_sem.at[3]),
    ]
    pl.semaphore_wait(barrier, n - 1)

    def zone(chunk):
        return pl.ds(pl.multiple_of(PAD + chunk * rows, 8), rows)

    def halo_copy(level, chunk, side, first):
        start = 0 if side == 0 else layers - HALO
        if first:
            source = now_hbm.at[
                pl.ds(start, HALO), pl.ds(pl.multiple_of(chunk * rows, 8), rows), :
            ]
        else:
            source = field.at[level, pl.ds(HALO + start, HALO), zone(chunk), :]
        landing = HALO + layers if side == 0 else 0
        other = me - 1 if side == 0 else me + 1
        other = jnp.clip(other, 0, n - 1)
        return pltpu.make_async_remote_copy(
            src_ref=source,
            dst_ref=field.at[level, pl.ds(landing, HALO), zone(chunk), :],
            send_sem=send_sem.at[level, side, chunk],
            recv_sem=recv_sem.at[level, side, chunk],
            device_id=(shot, other),
            device_id_type=MESH,
        )

    has_left = me > 0
    has_right = me < n - 1

    def start_halo(level, chunk, first=False):
        @pl.when(has_left)
        def _():
            halo_copy(level, chunk, 0, first).start()

        @pl.when(has_right)
        def _():
            halo_copy(level, chunk, 1, first).start()

    for chunk in range(CHUNKS):
        start_halo(1, chunk, True)
    for load in loads:
        load.start()

    packed = pack_traces(
        n, residual[...], owner[...], cell[...], cluster[...], gain[...], width
    )
    for device in range(n):
        outbox[device] = packed[device : device + 1, :]

    def mail(i):
        other = lax.rem(me + i, n)
        return pltpu.make_async_remote_copy(
            src_ref=outbox.at[other],
            dst_ref=inbox.at[me],
            send_sem=mail_send.at[i],
            recv_sem=mail_recv.at[i],
            device_id=(shot, other),
            device_id_type=MESH,
        )

    def mail_from(i):
        other = lax.rem(me + n - i, n)
        return pltpu.make_async_remote_copy(
            src_ref=outbox.at[other],
            dst_ref=inbox.at[other],
            send_sem=mail_send.at[i],
            recv_sem=mail_recv.at[i],
            device_id=(shot, other),
            device_id_type=MESH,
        )

    @pl.loop(1, n)
    def _(i):
        mail(i).start()

    inbox[me] = outbox[me]

    blank = jnp.zeros((layers, PAD, width), jnp.float32)
    for level in range(1, STEPS + 1):
        field[level, pl.ds(HALO, layers), pl.ds(0, PAD), :] = blank
        field[level, pl.ds(HALO, layers), pl.ds(PAD + depth, PAD), :] = blank
    edge = jnp.zeros((HALO, depth, width), jnp.float32)

    @pl.when(jnp.logical_not(has_left))
    def _():
        @pl.loop(1, STEPS + 1)
        def _(level):
            field[level, pl.ds(0, HALO), pl.ds(PAD, depth), :] = edge

    @pl.when(jnp.logical_not(has_right))
    def _():
        @pl.loop(1, STEPS + 1)
        def _(level):
            field[level, pl.ds(HALO + layers, HALO), pl.ds(PAD, depth), :] = edge

    @pl.loop(1, n)
    def _(i):
        mail_from(i).wait_recv()

    arrived = jnp.concatenate(
        [jnp.broadcast_to(inbox[device], (CAP, LANES)) for device in range(n)], axis=0
    )
    lane = iota((slots, LANES), 1)
    own_slot = iota((slots, LANES), 0) % CAP

    def pick(number):
        chosen = jnp.where(lane == number * CAP + own_slot, arrived, 0.0)
        return jnp.sum(chosen, axis=1, keepdims=True)

    for step in range(STEPS):
        rest = pick(step)
        for part in range(3):
            piece = rest.astype(jnp.bfloat16).astype(jnp.float32)
            parts[step, :, part : part + 1] = piece
            rest = rest - piece
    target_row = jnp.broadcast_to(pick(STEPS), (slots, LANES)).T[0:1, :].astype(jnp.int32)
    row_hot[...] = jnp.where(target_row == iota((layers * depth, slots), 0), 1.0, 0.0).astype(
        jnp.bfloat16
    )
    columns[...] = jnp.broadcast_to(pick(STEPS + 1), (slots, LANES)).astype(jnp.int32)

    for load in loads:
        load.wait()

    centre_weight = 3.0 * stencil_weights[0]

    @pl.loop(0, STEPS)
    def _(step):
        level = step + 1
        total = None
        hit = columns[:, 0:1] == iota((slots, width), 1)
        for part in range(3):
            values = jnp.where(hit, parts[step, :, part : part + 1], 0.0).astype(jnp.bfloat16)
            product = jnp.dot(row_hot[...], values, preferred_element_type=jnp.float32)
            total = product if total is None else total + product
        added[...] = total

        @pl.loop(0, CHUNKS)
        def _(chunk):
            here = zone(chunk)
            plain = pl.ds(pl.multiple_of(chunk * rows, 8), rows)
            window = pl.ds(pl.multiple_of(chunk * rows, 8), rows + 2 * PAD)

            @pl.when(has_left)
            def _():
                halo_copy(level, chunk, 1, False).wait_recv()

            @pl.when(has_right)
            def _():
                halo_copy(level, chunk, 0, False).wait_recv()

            lane = iota((rows, width), 1)

            @pl.loop(0, layers)
            def _(x):
                place = x + HALO
                strip = field[level, place, window, :]
                centre = strip[PAD : PAD + rows]
                summed = centre_weight * centre
                for m in range(1, 5):
                    pair = field[level, place + m, here, :] + field[level, place - m, here, :]
                    pair = pair + strip[PAD + m : PAD + m + rows] + strip[PAD - m : PAD - m + rows]
                    pair = pair + jnp.where(lane >= m, pltpu.roll(centre, m, 1), 0.0)
                    pair = pair + jnp.where(
                        lane < width - m, pltpu.roll(centre, width - m, 1), 0.0
                    )
                    summed = summed + stencil_weights[m] * pair
                speed = time_ratio * velocity[x, plain, :]
                following = 2.0 * centre - field[level - 1, place, here, :]
                following = following + (speed * speed) * summed
                following = following + added[
                    pl.ds(pl.multiple_of(x * depth + chunk * rows, 8), rows), :
                ]
                field[level + 1, place, here, :] = following
                change = (
                    fwd[step, x, plain, :]
                    - 2.0 * fwd[step + 1, x, plain, :]
                    + fwd[step + 2, x, plain, :]
                )
                term = centre * change

                @pl.when(step == 0)
                def _():
                    image[x, plain, :] = term

                @pl.when(step > 0)
                def _():
                    image[x, plain, :] = image[x, plain, :] + term

            @pl.when(step < STEPS - 1)
            def _():
                start_halo(level + 1, chunk)

    own = pl.ds(HALO, layers)
    inner = pl.ds(PAD, depth)
    stores = [
        pltpu.make_async_copy(field.at[STEPS, own, inner, :], older_hbm, out_sem.at[0]),
        pltpu.make_async_copy(field.at[STEPS + 1, own, inner, :], newer_hbm, out_sem.at[1]),
        pltpu.make_async_copy(image, image_hbm, out_sem.at[2]),
    ]
    for store in stores:
        store.start()

    @pl.loop(1, n)
    def _(i):
        mail(i).wait_send()

    def wait_halo(level, chunk, first):
        @pl.when(has_left)
        def _():
            halo_copy(level, chunk, 0, first).wait_send()

        @pl.when(has_right)
        def _():
            halo_copy(level, chunk, 1, first).wait_send()

    for chunk in range(CHUNKS):
        wait_halo(1, chunk, True)

    @pl.loop(2, STEPS + 1)
    def _(level):
        @pl.loop(0, CHUNKS)
        def _(chunk):
            wait_halo(level, chunk, False)

    for store in stores:
        store.wait()


def per_device(
    fwd_fields,
    velocity,
    adj_prev,
    adj_now,
    residual,
    rec_owner,
    rec_cell,
    rec_cluster,
    cluster_gain,
):
    n = lax.axis_size("gx")
    layers, depth, width = adj_now.shape
    traces = residual.shape[1]
    slots = n * CAP
    clusters = cluster_gain.shape[0]
    block = jax.ShapeDtypeStruct(adj_now.shape, jnp.float32)
    hbm = pl.BlockSpec(memory_space=pl.ANY)
    vmem = pl.BlockSpec(memory_space=pltpu.VMEM)
    older, newer, image = pl.pallas_call(
        functools.partial(kernel, n),
        out_shape=(block, block, block),
        in_specs=[hbm] * 4 + [vmem] * 5,
        out_specs=(hbm, hbm, hbm),
        scratch_shapes=[
            pltpu.VMEM(
                (STEPS + 2, layers + 2 * HALO, depth + 2 * PAD, width), jnp.float32
            ),
            pltpu.VMEM(fwd_fields.shape, jnp.float32),
            pltpu.VMEM(velocity.shape, jnp.float32),
            pltpu.VMEM(adj_now.shape, jnp.float32),
            pltpu.VMEM((layers * depth, width), jnp.float32),
            pltpu.VMEM((n, 1, LANES), jnp.float32),
            pltpu.VMEM((n, 1, LANES), jnp.float32),
            pltpu.VMEM((layers * depth, slots), jnp.bfloat16),
            pltpu.VMEM((slots, LANES), jnp.int32),
            pltpu.VMEM((STEPS, slots, LANES), jnp.float32),
            pltpu.SemaphoreType.DMA((4,)),
            pltpu.SemaphoreType.DMA((3,)),
            pltpu.SemaphoreType.DMA((STEPS + 1, 2, CHUNKS)),
            pltpu.SemaphoreType.DMA((STEPS + 1, 2, CHUNKS)),
            pltpu.SemaphoreType.DMA((n,)),
            pltpu.SemaphoreType.DMA((n,)),
        ],
        compiler_params=pltpu.CompilerParams(
            collective_id=0, has_side_effects=True, vmem_limit_bytes=48 * 1024 * 1024
        ),
        name="adjoint",
    )(
        fwd_fields,
        velocity,
        adj_prev,
        adj_now,
        residual,
        rec_owner.reshape(1, traces),
        rec_cell.reshape(1, traces),
        rec_cluster.reshape(1, traces),
        cluster_gain.reshape(clusters, 1),
    )
    return (older, newer, (2.0 / velocity) * image)


def solution(mesh):
    in_specs = (
        P(None, ("shot", "gx"), None, None),
        P("gx", None, None),
        P(("shot", "gx"), None, None),
        P(("shot", "gx"), None, None),
        P(None, ("shot", "gx")),
        P("gx", None),
        P("gx"),
        P("gx"),
        P(),
    )
    out_specs = (
        P(("shot", "gx"), None, None),
        P(("shot", "gx"), None, None),
        P(("shot", "gx"), None, None),
    )
    return jax.shard_map(
        per_device, mesh=mesh, in_specs=in_specs, out_specs=out_specs, check_vma=False
    )
```

time: 150 us -> 69.6 us (0.46); the launches traced: 147 us -> 69.3 us
  Pallas kernels: 0 us -> 59.6 us
  local copies, waits for them, and re-layouts: 43.8 us -> 7.85 us
  other arithmetic: 34.6 us -> 1.19 us
  starting transfers between devices: 32.4 us -> 0 us
  blocking collectives: 30.4 us -> 0 us
  waiting for transfers between devices: 4.99 us -> 0 us
    pallas_call x0 -> x1, Pallas kernels: none -> 59.6 us  [per_device(): pl.pallas_call(functools.partial(kernel, n), out_shape=(block, block, blo...]
    all_to_all x3 -> x0, blocking collectives: 30.4 us -> none  [per_device(): lax.all_to_all(send_values[:, :, step], 'gx', split_axis=0, concat_axis=0...]
    ppermute x8 -> x0, starting transfers between devices: 20 us -> none  [the longest x4 11.4 us: with_halo(): before = lax.ppermute(last, axis, up)]
    slice x12 -> x0, local copies, waits for them, and re-layouts: 19.6 us -> none  [the longest x7 13.5 us: with_halo(): initial = lax.slice_in_dim(shard, 0, width, axis=dim)]
    add x5 -> x0, other arithmetic: 15.7 us -> none  [the longest x4 10.1 us: per_device(): following = 2.0 * newer - older + courant * laplace(extended)]
    scatter-add x4 -> x0, other arithmetic: 12.9 us -> none  [inject(): flat = wave_field.reshape(-1).at[cells_in].add(values)]
    all_to_all x2 -> x0, starting transfers between devices: 12.4 us -> none  [the longest x1 6.61 us: per_device(): lax.all_to_all(send_cells, 'gx', split_axis=0, concat_axis=0, tiled=True)]
    reshape x9 -> x1, local copies, waits for them, and re-layouts: 7.64 us -> 0.74 us  [per_device(): cluster_gain.reshape(clusters, 1)]
  transfers between devices with their start and end apart: 10 -> 0, of which waited for: 2 -> 0; matrix products, arithmetic and copies ran while one was open for 21% -> 0% of each run, Pallas kernels for 0% -> 0%
where the time goes in v1:
time: 69.6 us; the launch traced here: 69.3 us
  Pallas kernels  59.6 us (86%)
  local copies, waits for them, and re-layouts  7.85 us (11%)
  other arithmetic  1.19 us (2%)
    pallas_call x1, Pallas kernels, per_device(): pl.pallas_call(functools.partial(kernel, n), out_shape=(block, block, blo...  59.6 us
    unnamed x14, local copies, waits for them, and re-layouts  7.11 us

profile of v1, /device:TPU:9, one launch (start us, length us, event | category | flops | bytes accessed | tf_op | source)
XLA Modules:
  0.0 69.3 jit_solution(9029664657909076225)
XLA Ops:
  0.6 0.7 %copy.12.gain = f32[32,1]{1,0:T(8,128)S(1)} copy(f32[32,1]{0,1:T(1,128)} %bitcast.7) | data formatting | bytes 256 | tf_op jit(solution)/shard_map/reshape | solution.py:405
  1.4 0.0 copy-start
  1.4 1.2 %copy-done = f32[8,64,512]{2,1,0:T(8,128)S(1)} copy-done((f32[8,64,512]{2,1,0:T(8,128)S(1)}, f32[8,64,512]{2,1,0:T(8,128)}, u32[]{:S(2)}) %copy-start) | copy-done | bytes 1048600
  2.6 0.0 copy-start.1
  2.6 1.2 %copy-done.1 = f32[8,64,512]{2,1,0:T(8,128)S(1)} copy-done((f32[8,64,512]{2,1,0:T(8,128)S(1)}, f32[8,64,512]{2,1,0:T(8,128)}, u32[]{:S(2)}) %copy-start.1) | copy-done | bytes 1048600
  3.8 0.0 copy-start.2
  3.8 0.7 copy-done.2
  4.5 0.0 copy-start.3
  4.5 0.7 copy-done.3
  5.2 0.0 copy-start.4
  5.2 0.7 copy-done.4
  5.9 0.0 copy-start.5
  5.9 0.7 copy-done.5
  6.5 59.6 %adjoint.1 = (f32[8,64,512]{2,1,0:T(8,128)S(1)}, f32[8,64,512]{2,1,0:T(8,128)S(1)}, f32[8,64,512]{2,1,0:T(8,128)S(1)}) custom-call(f32[6,8,64,512]{3,2,1,0:T(8,128)} %fwd_hbm.1, f32[8,64,512]{2,1,0:T(8,128)S(1)} %copy-done, f32[8,64,512]{2,1,0:T(8,128)S(1)} %copy-done.1, f32[8,64,512]{2,1,0:T(8,128)} %now_hbm.1, f32[4,256]{1,0:T(4,128)S(1)} %copy-done.2, ...), custom_call_target="tpu_custom_call" | custom-call | tf_op jit(solution)/shard_map/adjoint/pallas_call | solution.py:367
  66.2 1.2 %divide_multiply_fusion = f32[8,64,512]{2,1,0:T(8,128)} fusion(f32[8,64,512]{2,1,0:T(8,128)S(1)} %get-tuple-element.8, f32[8,64,512]{2,1,0:T(8,128)S(1)} %copy-done), kind=kLoop, calls=%fused_computation | loop fusion | flops 524288 | bytes 3145728 | tf_op jit(solution)/shard_map/mul | solution.py:407
  67.4 1.0 %copy.15 = f32[8,64,512]{2,1,0:T(8,128)} copy(f32[8,64,512]{2,1,0:T(8,128)S(1)} %get-tuple-element.12) | data formatting | bytes 2097152
  68.3 1.0 %copy.16 = f32[8,64,512]{2,1,0:T(8,128)} copy(f32[8,64,512]{2,1,0:T(8,128)S(1)} %get-tuple-element.13) | data formatting | bytes 2097152
Async XLA Ops:
  1.4 1.2 %copy-start = (f32[8,64,512]{2,1,0:T(8,128)S(1)}, f32[8,64,512]{2,1,0:T(8,128)}, u32[]{:S(2)}) copy-start(f32[8,64,512]{2,1,0:T(8,128)} %velocity_hbm.1) | copy-start | bytes 3145732
  2.6 1.2 %copy-start.1 = (f32[8,64,512]{2,1,0:T(8,128)S(1)}, f32[8,64,512]{2,1,0:T(8,128)}, u32[]{:S(2)}) copy-start(f32[8,64,512]{2,1,0:T(8,128)} %prev_hbm.1) | copy-start | bytes 3145732
  3.8 0.7 copy-start.2
  4.5 0.7 copy-start.3
  5.2 0.7 copy-start.4
  5.9 0.7 copy-start.5

commit v2 on v1

--- a/solution.py
+++ b/solution.py
@@ -10,10 +10,12 @@
 STEPS = 4
 CAP = 16
 CHUNKS = 4
+PIECES = 3
 PAD = 8
 HALO = 4
 LANES = 128
 FIELDS = 6
+VMEM_BYTES = 62 * 1024 * 1024
 MESH = pl.DeviceIdType.MESH
 
 stencil_weights = (-205.0 / 72.0, 8.0 / 5.0, -1.0 / 5.0, 8.0 / 315.0, -1.0 / 560.0)
@@ -26,7 +28,10 @@
 
 def pack_traces(n, residual, owner, cell, cluster, gain, width):
     traces = residual.shape[1]
-    clusters = gain.shape[0]
+    clusters = gain.shape[1]
+    square = (clusters, clusters)
+    gain = jnp.where(iota(square, 0) == iota(square, 1), gain, 0.0)
+    gain = jnp.sum(gain, axis=1, keepdims=True)
     picked = cluster == iota((clusters, traces), 0)
     gains = jnp.sum(jnp.where(picked, gain, 0.0), axis=0, keepdims=True)
     amplitude = residual * gains
@@ -68,11 +73,11 @@
     velocity_hbm,
     prev_hbm,
     now_hbm,
-    residual,
-    owner,
-    cell,
-    cluster,
-    gain,
+    residual_hbm,
+    owner_hbm,
+    cell_hbm,
+    cluster_hbm,
+    gain_hbm,
     older_hbm,
     newer_hbm,
     image_hbm,
@@ -86,6 +91,12 @@
     row_hot,
     columns,
     parts,
+    band,
+    residual,
+    owner,
+    cell,
+    cluster,
+    gain,
     load_sem,
     out_sem,
     send_sem,
@@ -107,6 +118,13 @@
             barrier, inc=1, device_id=(shot, lax.rem(me + i, n)), device_id_type=MESH
         )
 
+    tables = [
+        pltpu.make_async_copy(residual_hbm, residual, load_sem.at[4]),
+        pltpu.make_async_copy(owner_hbm, owner, load_sem.at[5]),
+        pltpu.make_async_copy(cell_hbm, cell, load_sem.at[6]),
+        pltpu.make_async_copy(cluster_hbm, cluster, load_sem.at[7]),
+        pltpu.make_async_copy(gain_hbm, gain, load_sem.at[8]),
+    ]
     loads = [
         pltpu.make_async_copy(
             now_hbm, field.at[1, pl.ds(HALO, layers), pl.ds(PAD, depth), :], load_sem.at[0]
@@ -117,6 +135,17 @@
         pltpu.make_async_copy(velocity_hbm, velocity, load_sem.at[2]),
         pltpu.make_async_copy(fwd_hbm, fwd, load_sem.at[3]),
     ]
+    for load in tables + loads:
+        load.start()
+    for load in tables:
+        load.wait()
+
+    packed = pack_traces(
+        n, residual[...], owner[...], cell[...], cluster[...], gain[...], width
+    )
+    for device in range(n):
+        outbox[device] = packed[device : device + 1, :]
+
     pl.semaphore_wait(barrier, n - 1)
 
     def zone(chunk):
@@ -154,16 +183,14 @@
         def _():
             halo_copy(level, chunk, 1, first).start()
 
-    for chunk in range(CHUNKS):
-        start_halo(1, chunk, True)
-    for load in loads:
-        load.start()
-
-    packed = pack_traces(
-        n, residual[...], owner[...], cell[...], cluster[...], gain[...], width
-    )
-    for device in range(n):
-        outbox[device] = packed[device : device + 1, :]
+    def wait_halo(level, chunk, first=False):
+        @pl.when(has_left)
+        def _():
+            halo_copy(level, chunk, 0, first).wait_send()
+
+        @pl.when(has_right)
+        def _():
+            halo_copy(level, chunk, 1, first).wait_send()
 
     def mail(i):
         other = lax.rem(me + i, n)
@@ -192,7 +219,16 @@
         mail(i).start()
 
     inbox[me] = outbox[me]
-
+    for chunk in range(0, CHUNKS):
+        start_halo(1, chunk, True)
+
+
+    image[...] = jnp.zeros_like(image)
+    apart = jnp.abs(iota((width, width), 0) - iota((width, width), 1))
+    weights = jnp.zeros((width, width), jnp.float32)
+    for m, whole in ((1, 8064.0), (2, -1008.0), (3, 128.0), (4, -9.0)):
+        weights = jnp.where(apart == m, whole, weights)
+    band[...] = weights.astype(jnp.bfloat16)
     blank = jnp.zeros((layers, PAD, width), jnp.float32)
     for level in range(1, STEPS + 1):
         field[level, pl.ds(HALO, layers), pl.ds(0, PAD), :] = blank
@@ -241,18 +277,22 @@
         load.wait()
 
     centre_weight = 3.0 * stencil_weights[0]
-
-    @pl.loop(0, STEPS)
-    def _(step):
-        level = step + 1
+    y_scale = 1.0 / 5040.0
+
+    def sum_traces(step):
         total = None
         hit = columns[:, 0:1] == iota((slots, width), 1)
         for part in range(3):
             values = jnp.where(hit, parts[step, :, part : part + 1], 0.0).astype(jnp.bfloat16)
             product = jnp.dot(row_hot[...], values, preferred_element_type=jnp.float32)
             total = product if total is None else total + product
-        added[...] = total
-
+        added[step % 2] = total
+
+    sum_traces(0)
+
+    @pl.loop(0, STEPS)
+    def _(step):
+        level = step + 1
         @pl.loop(0, CHUNKS)
         def _(chunk):
             here = zone(chunk)
@@ -267,27 +307,28 @@
             def _():
                 halo_copy(level, chunk, 0, False).wait_recv()
 
-            lane = iota((rows, width), 1)
-
-            @pl.loop(0, layers)
-            def _(x):
+            rest = field[level, pl.ds(HALO, layers), here, :].reshape(layers * rows, width)
+            across = None
+            for part in range(PIECES):
+                piece = rest.astype(jnp.bfloat16)
+                product = jnp.dot(piece, band[...], preferred_element_type=jnp.float32)
+                across = product if across is None else across + product
+                rest = rest - piece.astype(jnp.float32)
+
+            for x in range(layers):
                 place = x + HALO
                 strip = field[level, place, window, :]
                 centre = strip[PAD : PAD + rows]
-                summed = centre_weight * centre
+                summed = centre_weight * centre + y_scale * across[x * rows : (x + 1) * rows]
                 for m in range(1, 5):
                     pair = field[level, place + m, here, :] + field[level, place - m, here, :]
                     pair = pair + strip[PAD + m : PAD + m + rows] + strip[PAD - m : PAD - m + rows]
-                    pair = pair + jnp.where(lane >= m, pltpu.roll(centre, m, 1), 0.0)
-                    pair = pair + jnp.where(
-                        lane < width - m, pltpu.roll(centre, width - m, 1), 0.0
-                    )
                     summed = summed + stencil_weights[m] * pair
                 speed = time_ratio * velocity[x, plain, :]
                 following = 2.0 * centre - field[level - 1, place, here, :]
                 following = following + (speed * speed) * summed
                 following = following + added[
-                    pl.ds(pl.multiple_of(x * depth + chunk * rows, 8), rows), :
+                    step % 2, pl.ds(pl.multiple_of(x * depth + chunk * rows, 8), rows), :
                 ]
                 field[level + 1, place, here, :] = following
                 change = (
@@ -297,17 +338,15 @@
                 )
                 term = centre * change
 
-                @pl.when(step == 0)
-                def _():
-                    image[x, plain, :] = term
-
-                @pl.when(step > 0)
-                def _():
-                    image[x, plain, :] = image[x, plain, :] + term
+                image[x, plain, :] = image[x, plain, :] + term
 
             @pl.when(step < STEPS - 1)
             def _():
                 start_halo(level + 1, chunk)
+
+            @pl.when(jnp.logical_and(step < STEPS - 1, chunk == 1))
+            def _():
+                sum_traces(step + 1)
 
     own = pl.ds(HALO, layers)
     inner = pl.ds(PAD, depth)
@@ -323,23 +362,14 @@
     def _(i):
         mail(i).wait_send()
 
-    def wait_halo(level, chunk, first):
-        @pl.when(has_left)
-        def _():
-            halo_copy(level, chunk, 0, first).wait_send()
-
-        @pl.when(has_right)
-        def _():
-            halo_copy(level, chunk, 1, first).wait_send()
-
-    for chunk in range(CHUNKS):
+    for chunk in range(0, CHUNKS):
         wait_halo(1, chunk, True)
 
     @pl.loop(2, STEPS + 1)
     def _(level):
         @pl.loop(0, CHUNKS)
         def _(chunk):
-            wait_halo(level, chunk, False)
+            wait_halo(level, chunk)
 
     for store in stores:
         store.wait()
@@ -357,17 +387,17 @@
     cluster_gain,
 ):
     n = lax.axis_size("gx")
-    layers, depth, width = adj_now.shape
+    width = adj_now.shape[2]
+    layers, depth = adj_now.shape[:2]
     traces = residual.shape[1]
     slots = n * CAP
     clusters = cluster_gain.shape[0]
     block = jax.ShapeDtypeStruct(adj_now.shape, jnp.float32)
-    hbm = pl.BlockSpec(memory_space=pl.ANY)
-    vmem = pl.BlockSpec(memory_space=pltpu.VMEM)
+    hbm = pl.BlockSpec(memory_space=pltpu.HBM)
     older, newer, image = pl.pallas_call(
         functools.partial(kernel, n),
         out_shape=(block, block, block),
-        in_specs=[hbm] * 4 + [vmem] * 5,
+        in_specs=[hbm] * 9,
         out_specs=(hbm, hbm, hbm),
         scratch_shapes=[
             pltpu.VMEM(
@@ -376,13 +406,19 @@
             pltpu.VMEM(fwd_fields.shape, jnp.float32),
             pltpu.VMEM(velocity.shape, jnp.float32),
             pltpu.VMEM(adj_now.shape, jnp.float32),
-            pltpu.VMEM((layers * depth, width), jnp.float32),
+            pltpu.VMEM((2, layers * depth, width), jnp.float32),
             pltpu.VMEM((n, 1, LANES), jnp.float32),
             pltpu.VMEM((n, 1, LANES), jnp.float32),
             pltpu.VMEM((layers * depth, slots), jnp.bfloat16),
             pltpu.VMEM((slots, LANES), jnp.int32),
             pltpu.VMEM((STEPS, slots, LANES), jnp.float32),
-            pltpu.SemaphoreType.DMA((4,)),
+            pltpu.VMEM((width, width), jnp.bfloat16),
+            pltpu.VMEM(residual.shape, jnp.float32),
+            pltpu.VMEM((1, traces), jnp.int32),
+            pltpu.VMEM((1, traces), jnp.int32),
+            pltpu.VMEM((1, traces), jnp.int32),
+            pltpu.VMEM((1, clusters), jnp.float32),
+            pltpu.SemaphoreType.DMA((9,)),
             pltpu.SemaphoreType.DMA((3,)),
             pltpu.SemaphoreType.DMA((STEPS + 1, 2, CHUNKS)),
             pltpu.SemaphoreType.DMA((STEPS + 1, 2, CHUNKS)),
@@ -390,7 +426,7 @@
             pltpu.SemaphoreType.DMA((n,)),
         ],
         compiler_params=pltpu.CompilerParams(
-            collective_id=0, has_side_effects=True, vmem_limit_bytes=48 * 1024 * 1024
+            collective_id=0, has_side_effects=True, vmem_limit_bytes=VMEM_BYTES
         ),
         name="adjoint",
     )(
@@ -402,7 +438,7 @@
         rec_owner.reshape(1, traces),
         rec_cell.reshape(1, traces),
         rec_cluster.reshape(1, traces),
-        cluster_gain.reshape(clusters, 1),
+        cluster_gain.reshape(1, clusters),
     )
     return (older, newer, (2.0 / velocity) * image)
 

time: 69.6 us -> 63.3 us (0.909); the launches traced: 69.3 us -> 62.2 us
  Pallas kernels: 59.6 us -> 54.6 us
  local copies, waits for them, and re-layouts: 7.85 us -> 4.53 us
  other arithmetic: 1.19 us -> 2.42 us
    pallas_call x1, Pallas kernels: 59.6 us -> 54.6 us  [per_device(): pl.pallas_call(functools.partial(kernel, n), out_shape=(block, block, blo...]
    unnamed x14 -> x4, local copies, waits for them, and re-layouts: 7.11 us -> 4.53 us
    mul x1, other arithmetic: 1.19 us -> 2.42 us  [per_device(): return (older, newer, 2.0 / velocity * image)]
    reshape x1 -> x0, local copies, waits for them, and re-layouts: 0.74 us -> none  [per_device(): cluster_gain.reshape(clusters, 1)]
where the time goes in v2:
time: 63.3 us; the launch traced here: 62.2 us
  Pallas kernels  54.6 us (86%)
  local copies, waits for them, and re-layouts  4.53 us (7%)
  other arithmetic  2.42 us (4%)
  between operations  0.66 us (1%)
    pallas_call x1, Pallas kernels, per_device(): pl.pallas_call(functools.partial(kernel, n), out_shape=(block, block, blo...  54.6 us
    unnamed x4, local copies, waits for them, and re-layouts  4.53 us
    mul x1, other arithmetic, per_device(): return (older, newer, 2.0 / velocity * image)  2.42 us

profile of v2, /device:TPU:9, one launch (start us, length us, event | category | flops | bytes accessed | tf_op | source)
XLA Modules:
  0.0 62.2 jit_solution(6831848279609435483)
XLA Ops:
  0.6 0.0 copy-start
  0.6 54.6 %adjoint.1 = (f32[8,64,512]{2,1,0:T(8,128)}, f32[8,64,512]{2,1,0:T(8,128)}, f32[8,64,512]{2,1,0:T(8,128)}) custom-call(f32[6,8,64,512]{3,2,1,0:T(8,128)} %fwd_hbm.1, f32[8,64,512]{2,1,0:T(8,128)} %velocity_hbm.1, f32[8,64,512]{2,1,0:T(8,128)} %prev_hbm.1, f32[8,64,512]{2,1,0:T(8,128)} %now_hbm.1, f32[4,256]{1,0:T(4,128)} %residual_hbm.1, s32[1,256]{1,0:T(1,128)} %bitcast.4, ...), custom_call_target="tpu_custom_call" | custom-call | tf_op jit(solution)/shard_map/adjoint/pallas_call | solution.py:397
  55.2 0.0 copy-done
  55.2 2.4 %divide_multiply_fusion = f32[8,64,512]{2,1,0:T(8,128)} fusion(f32[8,64,512]{2,1,0:T(8,128)} %get-tuple-element.8, f32[8,64,512]{2,1,0:T(8,128)S(1)} %copy-done), kind=kLoop, calls=%fused_computation | loop fusion | flops 524288 | bytes 3145728 | tf_op jit(solution)/shard_map/mul | solution.py:443
  57.6 2.3 %copy.14 = f32[8,64,512]{2,1,0:T(8,128)} copy(f32[8,64,512]{2,1,0:T(8,128)} %get-tuple-element.12) | data formatting | bytes 2097152
  59.9 2.3 %copy.15 = f32[8,64,512]{2,1,0:T(8,128)} copy(f32[8,64,512]{2,1,0:T(8,128)} %get-tuple-element.13) | data formatting | bytes 2097152
Async XLA Ops:
  0.6 54.6 %copy-start = (f32[8,64,512]{2,1,0:T(8,128)S(1)}, f32[8,64,512]{2,1,0:T(8,128)}, u32[]{:S(2)}) copy-start(f32[8,64,512]{2,1,0:T(8,128)} %velocity_hbm.1) | copy-start | bytes 3145732
